TPU v7x, 256 devices: a whole 4x4x8 slice. The times are simulated.
256 devices in a mesh: row: 32 (over x, y, core), col: 8 (over z).
Axes of the slice: x: 4, y: 4, z: 8, core: 2. Of those that a mesh axis runs over, the one named last changes fastest.
Arguments:
- panel: float32 [32768, 256], P(('row', 'col')), may hold values from -8 to 8
- diag_inverse: float32 [256, 256], replicated
- tiles: bfloat16 [10240, 256, 256], P(('row', 'col')), may hold values from -6 to 6
- tile_map: int32 [10240, 2], P(('row', 'col')), may hold values from -1 to 15, as said below
- send_list: int32 [1536], P(('row', 'col')), may hold values from -1 to 39, as said below
- place_list: int32 [8704], P(('row', 'col')), may hold values from -1 to 45, as said below
Outputs:
- factor_panel: float32 [32768, 256], P(('row', 'col'))
- balanced: bfloat16 [8704, 256, 256], P(('row', 'col'))
Inputs may be any that keep to these rules, and one draw needn't show every extreme that they name: `tile_map`: each lower tile (I >= J) owned block-cyclically by a device appears in exactly one of its slots, in a drawn order; its other slots hold -1 in both entries. `send_list`: entries of a device name distinct live slots of that device, those it hands to its partner; unused entries are -1 and stand after the used ones. `place_list`: over a device's 34 entries, every live slot it does not hand over and every used send entry of its partner appear exactly once, in a drawn order; the rest are -1.
All inputs are finite; a program needn't handle non-finite values.
Results may differ from a plain program's by a relative error of at most 0.0051.
Values may be sent and summed in bfloat16 or wider, within the bound.
A program may use at most 128 MiB of HBM per device.

v0:
```python
import jax
import jax.numpy as jnp
from jax import lax
from jax.sharding import PartitionSpec as P


def swapped(value, axis, stride):
    mask = 2**stride
    pairs = [(source, source ^ mask) for source in range(lax.axis_size(axis))]
    return lax.ppermute(value, axis, pairs)


def pick_tiles(stack_tiles, index_list):
    return jnp.take(stack_tiles, index_list, axis=0)


def renew_tiles(raw_block, left_block, right_block):
    product = jnp.einsum(
        "sik,sjk->sij", left_block, right_block, preferred_element_type=jnp.float32
    )
    return (raw_block.astype(jnp.float32) - product).astype(jnp.bfloat16)


def shards(panel, diag_inverse, tiles, tile_map, send_list, place_list):
    slot_count = tiles.shape[0]
    tile_size = tiles.shape[1]
    move_count = send_list.shape[0]
    row_count = lax.axis_size("row")
    col_count = lax.axis_size("col")
    column = lax.axis_index("col")
    groups = row_count // col_count
    bit_count = row_count.bit_length() - 1
    zero_half = jnp.zeros((), jnp.bfloat16)
    send_valid = send_list >= 0
    send_safe = jnp.clip(send_list, 0, slot_count - 1)
    factor = jnp.dot(
        panel, diag_inverse.T, precision=lax.Precision.HIGHEST, preferred_element_type=jnp.float32
    )
    row_block = lax.all_gather(factor.astype(jnp.bfloat16), "col", axis=0, tiled=True)
    row_tiles = row_block.reshape(-1, tile_size, tile_size)
    row_local = row_tiles.shape[0]
    everything = lax.all_gather(row_tiles, "row", axis=0, tiled=True)
    shaped = everything.reshape(groups, col_count, row_local, tile_size, tile_size)
    picked = lax.dynamic_index_in_dim(shaped, column, 1, keepdims=False)
    col_tiles = picked.reshape(-1, tile_size, tile_size)
    row_pick = jnp.clip(tile_map[:, 0], 0, row_local - 1)
    col_pick = jnp.clip(tile_map[:, 1], 0, groups * row_local - 1)
    col_flat = col_pick % groups * row_local + col_pick // groups
    left_all = pick_tiles(row_tiles, row_pick)
    right_all = pick_tiles(col_tiles, col_flat)
    renewed_all = renew_tiles(tiles, left_all, right_all)
    outgoing_new = jnp.where(
        send_valid[:, None, None], pick_tiles(renewed_all, send_safe), zero_half
    )
    for bit_index in range(bit_count):
        outgoing_new = swapped(outgoing_new, "row", bit_index)
    tile_pool = jnp.concatenate([renewed_all, outgoing_new], 0)
    renewed = pick_tiles(tile_pool, jnp.clip(place_list, 0, slot_count + move_count - 1))
    balanced = jnp.where((place_list >= 0)[:, None, None], renewed, zero_half)
    return (factor, balanced)


def solution(mesh):
    in_specs = (
        P(("row", "col"), None),
        P(),
        P(("row", "col"), None, None),
        P(("row", "col"), None),
        P(("row", "col")),
        P(("row", "col")),
    )
    out_specs = (P(("row", "col"), None), P(("row", "col"), None, None))
    return jax.shard_map(shards, mesh=mesh, in_specs=in_specs, out_specs=out_specs, check_vma=False)
```

profile of v0, /device:TPU:1, one launch (start us, length us, event | category | flops | bytes accessed | tf_op | source)
XLA Modules:
  0.0 239.7 jit_solution(3499048586466523202)
XLA Ops:
  7.2 0.0 copy-start
  7.2 0.0 all-gather.2.cloned.1.call-start
  7.2 0.9 copy-done
  8.1 2.0 fusion.14
  10.1 26.3 %all_gather.6 = bf16[1024,256]{1,0:T(8,128)(2,1)} all-gather(bf16[128,256]{1,0:T(8,128)(2,1)S(1)} %get-tuple-element.11), channel_id=1, replica_groups=mesh['row'=32,'col'=8] {'col'}, dimensions={0}, use_global_device_ids=true | all-gather | bytes 589824 | tf_op jit(solution)/shard_map/all_gather | solution.py:39
  36.3 0.0 all-gather.2.cloned.1.call-update
  36.4 0.7 fusion.13
  37.1 0.0 copy-start.1
  37.1 0.0 copy-start.2
  37.1 5.6 %gather_fusion = bf16[40,256,256]{2,1,0:T(8,128)(2,1)} fusion(bf16[4,256,256]{2,1,0:T(8,128)(2,1)} %bitcast.13, s32[1024]{0:T(1024)S(1)} %pad_clamp_fusion.3), kind=kCustom, calls=%fused_computation | custom fusion | bytes 10485920 | tf_op jit(solution)/shard_map/jit(_take)/gather | solution.py:14
  42.7 0.0 copy-done.1
  42.7 0.0 copy-done.2
  42.8 76.7 %all-gather.2.cloned.1.call-done = bf16[128,256,256]{2,1,0:T(8,128)(2,1)} async-done(((bf16[4,256,256]{2,1,0:T(8,128)(2,1)}), bf16[128,256,256]{2,1,0:T(8,128)(2,1)}) %all-gather.2.cloned.1.call-update) | async-done | bytes 16777232 | tf_op jit(solution)/shard_map/all_gather | solution.py:42
  119.5 1.7 constant_dynamic-slice_fusion
  121.2 4.6 %gather_fusion.1 = bf16[40,256,256]{2,1,0:T(8,128)(2,1)} fusion(bf16[16,256,256]{2,1,0:T(8,128)(2,1)S(1)} %bitcast.14, s32[1024]{0:T(1024)S(1)} %pad_clamp_fusion.2), kind=kCustom, calls=%fused_computation.1 | custom fusion | bytes 10485920 | tf_op jit(solution)/shard_map/jit(_take)/gather | solution.py:14
  125.8 9.8 %subtract_convert_fusion = bf16[40,256,256]{2,1,0:T(8,128)(2,1)} fusion(bf16[40,256,256]{2,1,0:T(8,128)(2,1)} %param.8, bf16[40,256,256]{2,1,0:T(8,128)(2,1)} %gather_fusion.1, pred[40]{0:T(512)(128)(4,1)S(1)} %get-tuple-element.6, bf16[40,256,256]{2,1,0:T(8,128)(2,1)} %gather_fusion, pred[40]{0:T(512)(128)(4,1)S(1)} %get-tuple-element.8), kind=kOutput, calls=%fused_computation.4 | convolution fusion | flops 1355284480 | bytes 20971600 | tf_op jit(solution)/shard_map/sik,sjk->sij/dot_general | solution.py:18
  135.5 3.1 %gather_fusion.2 = bf16[6,256,256]{2,1,0:T(8,128)(2,1)S(1)} fusion(bf16[40,256,256]{2,1,0:T(8,128)(2,1)} %subtract_convert_fusion, s32[1024]{0:T(1024)S(1)} %pad_clamp_fusion.1), kind=kCustom, calls=%fused_computation.2 | custom fusion | bytes 1572888 | tf_op jit(solution)/shard_map/jit(_take)/gather | solution.py:14
  138.6 0.2 select_select_fusion.1
  138.8 0.3 collective-permute-start
  139.1 2.0 collective-permute-done
  141.2 0.8 collective-permute-start.1
  142.0 18.1 %collective-permute-done.1 = bf16[6,256,256]{2,1,0:T(8,128)(2,1)S(1)} collective-permute-done((bf16[6,256,256]{2,1,0:T(8,128)(2,1)S(1)}, bf16[6,256,256]{2,1,0:T(8,128)(2,1)S(1)}, u32[]{:S(2)}, u32[]{:S(2)}) %collective-permute-start.1) | collective-permute-done | bytes 786464 | tf_op jit(solution)/shard_map/ppermute | solution.py:10
  160.0 2.3 collective-permute-start.2
  162.4 17.1 %collective-permute-done.2 = bf16[6,256,256]{2,1,0:T(8,128)(2,1)S(1)} collective-permute-done((bf16[6,256,256]{2,1,0:T(8,128)(2,1)S(1)}, bf16[6,256,256]{2,1,0:T(8,128)(2,1)S(1)}, u32[]{:S(2)}, u32[]{:S(2)}) %collective-permute-start.2) | collective-permute-done | bytes 786464 | tf_op jit(solution)/shard_map/ppermute | solution.py:10
  179.5 1.1 collective-permute-start.3
  180.6 15.9 %collective-permute-done.3 = bf16[6,256,256]{2,1,0:T(8,128)(2,1)S(1)} collective-permute-done((bf16[6,256,256]{2,1,0:T(8,128)(2,1)S(1)}, bf16[6,256,256]{2,1,0:T(8,128)(2,1)S(1)}, u32[]{:S(2)}, u32[]{:S(2)}) %collective-permute-start.3) | collective-permute-done | bytes 786464 | tf_op jit(solution)/shard_map/ppermute | solution.py:10
  196.6 2.8 %collective-permute-start.4 = (bf16[6,256,256]{2,1,0:T(8,128)(2,1)S(1)}, bf16[6,256,256]{2,1,0:T(8,128)(2,1)S(1)}, u32[]{:S(2)}, u32[]{:S(2)}) collective-permute-start(bf16[6,256,256]{2,1,0:T(8,128)(2,1)S(1)} %collective-permute-done.3), channel_id=1, source_target_pairs={{0,128},{8,136},{16,144},{24,152},{32,160},{40,168},{48,176},{56,1... | collective-permute-start | bytes 2359304 | tf_op jit(solution)/shard_map/ppermute | solution.py:10
  199.3 0.0 copy-done.3
  199.4 15.9 %collective-permute-done.4 = bf16[6,256,256]{2,1,0:T(8,128)(2,1)S(1)} collective-permute-done((bf16[6,256,256]{2,1,0:T(8,128)(2,1)S(1)}, bf16[6,256,256]{2,1,0:T(8,128)(2,1)S(1)}, u32[]{:S(2)}, u32[]{:S(2)}) %collective-permute-start.4) | collective-permute-done | bytes 786464 | tf_op jit(solution)/shard_map/ppermute | solution.py:10
  215.2 5.6 %pad_maximum_fusion = bf16[46,256,256]{2,1,0:T(8,128)(2,1)} fusion(bf16[6,256,256]{2,1,0:T(8,128)(2,1)S(1)} %collective-permute-done.4, bf16[40,256,256]{2,1,0:T(8,128)(2,1)} %subtract_convert_fusion), kind=kLoop, calls=%fused_computation.5 | loop fusion | flops 3014656 | bytes 12058624 | tf_op jit(solution)/shard_map/concatenate | solution.py:57
  220.8 7.1 %gather_fusion.3 = bf16[34,256,256]{2,1,0:T(8,128)(2,1)} fusion(bf16[46,256,256]{2,1,0:T(8,128)(2,1)} %pad_maximum_fusion, s32[1024]{0:T(1024)S(1)} %pad_clamp_fusion), kind=kCustom, calls=%fused_computation.3 | custom fusion | bytes 8913032 | tf_op jit(solution)/shard_map/jit(_take)/gather | solution.py:14
  227.9 4.9 %select_select_fusion = bf16[34,256,256]{2,1,0:T(8,128)(2,1)} fusion(bf16[34,256,256]{2,1,0:T(8,128)(2,1)} %gather_fusion.3, pred[34]{0:T(512)(128)(4,1)S(1)} %get-tuple-element.2, pred[34]{0:T(512)(128)(4,1)S(1)} %get-tuple-element.9), kind=kLoop, calls=%fused_computation.11 | loop fusion | flops 4456448 | bytes 8912964 | tf_op jit(solution)/shard_map/jit(_where)/select_n | solution.py:59
  (8 shorter events, 0.1 us)
Async XLA Ops:
  7.2 1.0 copy-start
  7.2 112.3 %all-gather.2.cloned.1.call-start = ((), (), s32[]{:S(2)}) async-start(), calls=%async_computation | async-start | bytes 17301504 | tf_op jit(solution)/shard_map/all_gather | solution.py:42
  37.1 5.6 %copy-start.1 = (s32[40,2]{0,1:T(2,128)S(1)}, s32[40,2]{0,1:T(2,128)}, u32[]{:S(2)}) copy-start(s32[40,2]{0,1:T(2,128)} %param.9) | copy-start | bytes 964
  37.1 5.6 %copy-start.2 = (s32[6]{0:T(128)S(1)}, s32[6]{0:T(128)}, u32[]{:S(2)}) copy-start(s32[6]{0:T(128)} %param.10) | copy-start | bytes 76
  125.8 73.6 %copy-start.3 = (s32[34]{0:T(128)S(1)}, s32[34]{0:T(128)}, u32[]{:S(2)}) copy-start(s32[34]{0:T(128)} %param.11) | copy-start | bytes 412
  138.8 2.4 collective-permute-start
  141.2 18.9 %collective-permute-start.1 = (bf16[6,256,256]{2,1,0:T(8,128)(2,1)S(1)}, bf16[6,256,256]{2,1,0:T(8,128)(2,1)S(1)}, u32[]{:S(2)}, u32[]{:S(2)}) collective-permute-start(bf16[6,256,256]{2,1,0:T(8,128)(2,1)S(1)} %collective-permute-done), channel_id=1, source_target_pairs={{0,16},{8,24},{16,0},{24,8},{32,48},{40,56},{48,32},{56,40},{64,80... | collective-permute-start | bytes 2359304 | tf_op jit(solution)/shard_map/ppermute | solution.py:10
  160.0 19.5 %collective-permute-start.2 = (bf16[6,256,256]{2,1,0:T(8,128)(2,1)S(1)}, bf16[6,256,256]{2,1,0:T(8,128)(2,1)S(1)}, u32[]{:S(2)}, u32[]{:S(2)}) collective-permute-start(bf16[6,256,256]{2,1,0:T(8,128)(2,1)S(1)} %collective-permute-done.1), channel_id=1, source_target_pairs={{0,32},{8,40},{16,48},{24,56},{32,0},{40,8},{48,16},{56,24},{64,96... | collective-permute-start | bytes 2359304 | tf_op jit(solution)/shard_map/ppermute | solution.py:10
  179.5 17.0 %collective-permute-start.3 = (bf16[6,256,256]{2,1,0:T(8,128)(2,1)S(1)}, bf16[6,256,256]{2,1,0:T(8,128)(2,1)S(1)}, u32[]{:S(2)}, u32[]{:S(2)}) collective-permute-start(bf16[6,256,256]{2,1,0:T(8,128)(2,1)S(1)} %collective-permute-done.2), channel_id=1, source_target_pairs={{0,64},{8,72},{16,80},{24,88},{32,96},{40,104},{48,112},{56,120},{... | collective-permute-start | bytes 2359304 | tf_op jit(solution)/shard_map/ppermute | solution.py:10
  196.6 18.7 %collective-permute-start.4 = (bf16[6,256,256]{2,1,0:T(8,128)(2,1)S(1)}, bf16[6,256,256]{2,1,0:T(8,128)(2,1)S(1)}, u32[]{:S(2)}, u32[]{:S(2)}) collective-permute-start(bf16[6,256,256]{2,1,0:T(8,128)(2,1)S(1)} %collective-permute-done.3), channel_id=1, source_target_pairs={{0,128},{8,136},{16,144},{24,152},{32,160},{40,168},{48,176},{56,1... | collective-permute-start | bytes 2359304 | tf_op jit(solution)/shard_map/ppermute | solution.py:10
Sparse Core Ops, SparseCore 0:
  36.5 82.9 all-gather.1
where the time goes:
time: 241 us; the launch traced here: 240 us
  waiting for transfers between devices  146 us (61%)
  blocking collectives  26.3 us (11%)
  local copies, waits for them, and re-layouts  23 us (10%)
  between operations  14.1 us (6%)
  matrix products  11.7 us (5%)
  other arithmetic  11.4 us (5%)
  starting transfers between devices  7.42 us (3%)
    all_gather x1, waiting for transfers between devices, shards(): everything = lax.all_gather(row_tiles, 'row', axis=0, tiled=True)  76.7 us
    ppermute x5, waiting for transfers between devices, swapped(): return lax.ppermute(value, axis, pairs)  69 us
    all_gather x1, blocking collectives, shards(): lax.all_gather(factor.astype(jnp.bfloat16), 'col', axis=0, tiled=True)  26.3 us
    gather x4, local copies, waits for them, and re-layouts, pick_tiles(): return jnp.take(stack_tiles, index_list, axis=0)  20.3 us
    dot_general x1, matrix products, renew_tiles(): jnp.einsum('sik,sjk->sij', left_block, right_block, preferred_element_typ...  9.77 us
    ppermute x5, starting transfers between devices, swapped(): return lax.ppermute(value, axis, pairs)  7.38 us
    concatenate x1, other arithmetic, shards(): tile_pool = jnp.concatenate([renewed_all, outgoing_new], 0)  5.59 us
    select_n x1, other arithmetic, shards(): balanced = jnp.where((place_list >= 0)[:, None, None], renewed, zero_half)  4.92 us
  transfers between devices with their start and end apart: 6, of which 6 were waited for; matrix products, arithmetic and copies ran while one was open for 3% of the time, Pallas kernels for 0%

commit v1 on v0

v1 whole, which is shorter than its diff:
```python
import functools

import jax
import jax.numpy as jnp
from jax import lax
from jax.experimental import pallas as pl
from jax.experimental.pallas import tpu as pltpu
from jax.sharding import PartitionSpec as P

MESH = pl.DeviceIdType.MESH
NX, NY, NZ = 4, 4, 8
GROUPS = ((0,), (1, -1), (2, -2), (3, -3), (4,))
PIECE = {0: 0, 1: 1, -1: 2, 2: 3, -2: 4, 3: 5, -3: 6, 4: 7}
PARTNER_TICK = 4


class Ids:
    def __init__(self):
        self.count = 0

    def take(self, n):
        first = self.count
        self.count += n
        return first


SEND, RECV = Ids(), Ids()
S_ZP, S_ZM, S_QP, S_QM = (SEND.take(4) for _ in range(4))
S_PP, S_INFO = SEND.take(1), SEND.take(1)
S_EX = SEND.take(6)
S_YI, S_YC, S_YO, S_XC, S_XI, S_XF = (SEND.take(8) for _ in range(6))
S_DD = SEND.take(32)
R_ZP, R_ZM, R_QP, R_QM = (RECV.take(4) for _ in range(4))
R_PP, R_INFO = RECV.take(1), RECV.take(1)
R_EX = RECV.take(6)
R_AY, R_RC, R_RI, R_RF = (RECV.take(8) for _ in range(4))
R_DD = RECV.take(32)


def solve(panel, inverse):
    return lax.dot_general(
        panel,
        inverse,
        (((1,), (1,)), ((), ())),
        precision=lax.Precision.HIGHEST,
        preferred_element_type=jnp.float32,
    )


def gather_kernel(
    panel_ref, inv_ref, tiles_ref, map_ref, send_ref,
    rows_ref, cols_ref, recv_ref, info_ref,
    tile_buf, send_buf, half, info_src, send_sem, recv_sem, local_sem,
):
    r = lax.axis_index("row")
    z = lax.axis_index("col")
    x, y, k = r // 8, (r // 2) % 4, r % 2

    def dev(px, py, pk, pz):
        return (px * 8 + py * 2 + pk, pz)

    xi, xc = x + 1 - 2 * (x % 2), 3 - x
    yi, yc = y + 1 - 2 * (y % 2), 3 - y
    d_zp, d_zm = dev(x, y, k, (z + 1) % NZ), dev(x, y, k, (z + NZ - 1) % NZ)
    d_part = dev(3 - x, 3 - y, 1 - k, z)
    d_xi, d_xc = dev(xi, y, k, z), dev(xc, y, k, z)
    d_yi, d_yc = dev(x, yi, k, z), dev(x, yc, k, z)
    d_core = dev(x, y, 1 - k, z)
    sy, sk = z // 2, z % 2

    barrier = pltpu.get_barrier_semaphore()
    friends = (d_zp, d_zm, d_part, d_xi, d_xc, d_yi, d_yc, d_core)
    for friend in friends:
        pl.semaphore_signal(barrier, inc=1, device_id=friend, device_id_type=MESH)

    load = pltpu.make_async_copy(tiles_ref, tile_buf, local_sem.at[0])
    load.start()
    half[...] = solve(panel_ref[...], inv_ref[...]).astype(jnp.bfloat16)
    keep = pltpu.make_async_copy(half, rows_ref.at[z], local_sem.at[1])
    keep.start()

    def copy(src, dst, s, t, device):
        return pltpu.make_async_remote_copy(
            src_ref=src, dst_ref=dst, send_sem=send_sem.at[s], recv_sem=recv_sem.at[t],
            device_id=device, device_id_type=MESH,
        )

    def zpos(off):
        return (z + off + NZ) % NZ

    def ring(base, h, up, s0, t0, own):
        at = base + zpos(-h if up else h)
        device = d_zp if up else d_zm
        if h < 3:
            src = own if h == 0 else rows_ref.at[at]
            return copy(src, rows_ref.at[at], s0 + h, t0 + h, device)
        part = pl.ds(0, 64) if up else pl.ds(64, 64)
        return copy(rows_ref.at[at, part], rows_ref.at[at, part], s0 + h, t0 + h, device)

    def ring_send(base, h, s_up, s_down, r_up, r_down, own):
        ring(base, h, True, s_up, r_up, own).start()
        ring(base, h, False, s_down, r_down, own).start()

    def ring_wait_send(base, h, s_up, s_down, r_up, r_down, own):
        ring(base, h, True, s_up, r_up, own).wait_send()
        ring(base, h, False, s_down, r_down, own).wait_send()

    def ring_wait_recv(base, h, r_up, r_down):
        if h < 4:
            for off, t in ((-h, r_up), (h, r_down)):
                at = rows_ref.at[base + zpos(off)]
                copy(at, at, 0, t + h - 1, d_zp).wait_recv()
        else:
            for part, t in ((pl.ds(0, 64), r_up), (pl.ds(64, 64), r_down)):
                at = rows_ref.at[base + zpos(4), part]
                copy(at, at, 0, t + 3, d_zp).wait_recv()

    own_args = (0, S_ZP, S_ZM, R_ZP, R_ZM, half)
    part_args = (8, S_QP, S_QM, R_QP, R_QM, rows_ref.at[8 + z])

    def own_send(h, go="start"):
        b, su, sd, ru, rd, own = own_args
        (ring_send if go == "start" else ring_wait_send)(b, h, su, sd, ru, rd, own)

    def part_send(h, go="start"):
        b, su, sd, ru, rd, own = part_args
        (ring_send if go == "start" else ring_wait_send)(b, h, su, sd, ru, rd, own)

    partner_piece = copy(half, rows_ref.at[8 + z], S_PP, R_PP, d_part)
    partner_info = copy(info_src, info_ref, S_INFO, R_INFO, d_part)
    exchange = [
        copy(send_buf.at[j], recv_ref.at[j], S_EX + j, R_EX + j, d_part) for j in range(6)
    ]

    def cols_at(block, off):
        return cols_ref.at[block * 8 + zpos(off)]

    def mine(off, source):
        if not source:
            return cols_at(x, off)
        return half if off == 0 else rows_ref.at[zpos(off)]

    def y_in(off, source):
        i = PIECE[off]
        return copy(mine(off, source), cols_at(x, off), S_YI + i, R_AY + i, d_yi)

    def y_cross(off, source):
        i = PIECE[off]
        return copy(mine(off, source), cols_at(x, off), S_YC + i, R_AY + i, d_yc)

    def y_over(off):
        i = PIECE[off]
        return copy(cols_at(x, off), cols_at(x, off), S_YO + i, R_AY + i, d_yi)

    def x_cross(off, source):
        i = PIECE[off]
        return copy(mine(off, source), cols_at(x, off), S_XC + i, R_RC + i, d_xc)

    def x_in(off, source):
        i = PIECE[off]
        return copy(mine(off, source), cols_at(x, off), S_XI + i, R_RI + i, d_xi)

    def x_forward(off):
        i = PIECE[off]
        return copy(cols_at(xc, off), cols_at(xc, off), S_XF + i, R_RF + i, d_xi)

    def to_core(which, off, source):
        block = (x, xc, xi, 3 - xi)[which]
        i = which * 8 + PIECE[off]
        src = mine(off, source) if which == 0 else cols_at(block, off)
        return copy(src, cols_at(block, off), S_DD + i, R_DD + i, d_core)

    def arrived(ref, t):
        copy(ref, ref, 0, t, d_core).wait_recv()

    pl.semaphore_wait(barrier, len(friends))
    own_send(0)
    partner_piece.start()

    def sequence(depth, plane):
        source = depth == 0
        for t in range(0, 9):
            if 1 <= t <= 4:
                ring_wait_recv(0, t, R_ZP, R_ZM)
                if t <= 3:
                    own_send(t)
            p = t - PARTNER_TICK
            if p == 0:
                partner_piece.wait_recv()
                part_send(0)
            elif 1 <= p <= 4:
                ring_wait_recv(8, p, R_QP, R_QM)
                if p <= 3:
                    part_send(p)
            if not plane:
                continue
            g = t - depth
            if 0 <= g <= 4:
                for off in GROUPS[g]:
                    if not source:
                        arrived(cols_at(x, off), R_AY + PIECE[off])
                    if source:
                        y_cross(off, source).start()
                        y_in(off, source).start()
                    if depth == 1:
                        @pl.when(y == 3 - sy)
                        def _():
                            y_over(off).start()
                    x_cross(off, source).start()
                    x_in(off, source).start()
                    to_core(0, off, source).start()
            g = t - depth - 1
            if 0 <= g <= 4:
                for off in GROUPS[g]:
                    arrived(cols_at(xc, off), R_RC + PIECE[off])
                    x_forward(off).start()
                    to_core(1, off, source).start()
                for off in GROUPS[g]:
                    arrived(cols_at(xi, off), R_RI + PIECE[off])
                    to_core(2, off, source).start()
            g = t - depth - 2
            if 0 <= g <= 4:
                for off in GROUPS[g]:
                    arrived(cols_at(3 - xi, off), R_RF + PIECE[off])
                    to_core(3, off, source).start()
        if source:
            fill = pltpu.make_async_copy(
                rows_ref.at[pl.ds(0, 8)], cols_ref.at[pl.ds(x * 8, 8)], local_sem.at[2]
            )
            keep.wait()
            fill.start()
            fill.wait()
        if plane:
            for off in PIECE:
                if source:
                    y_in(off, source).wait_send()
                    y_cross(off, source).wait_send()
                if depth == 1:
                    @pl.when(y == 3 - sy)
                    def _():
                        y_over(off).wait_send()
                x_cross(off, source).wait_send()
                x_in(off, source).wait_send()
                x_forward(off).wait_send()
                for which in range(4):
                    to_core(which, off, source).wait_send()
        else:
            for which in range(4):
                block = (x, xc, xi, 3 - xi)[which]
                for off in PIECE:
                    arrived(cols_at(block, off), R_DD + which * 8 + PIECE[off])
        if not source:
            keep.wait()

    load.wait()
    lane = lax.broadcasted_iota(jnp.int32, (8, 128), 1)
    sub = lax.broadcasted_iota(jnp.int32, (8, 128), 0)
    info = jnp.zeros((8, 128), jnp.int32)
    for j in range(6):
        slot = jnp.clip(send_ref[j], 0, 39)
        send_buf[j] = tile_buf[slot]
        info = jnp.where((sub == j) & (lane == 0), map_ref[slot, 0], info)
        info = jnp.where((sub == j) & (lane == 1), map_ref[slot, 1], info)
    info_src[...] = info
    partner_info.start()
    for item in exchange:
        item.start()

    on_plane = k == sk
    is_source = y == sy
    is_far = y == (3 - sy) + 1 - 2 * ((3 - sy) % 2)

    @pl.when(on_plane & is_source)
    def _():
        sequence(0, True)

    @pl.when(on_plane & jnp.logical_not(is_source) & jnp.logical_not(is_far))
    def _():
        sequence(1, True)

    @pl.when(on_plane & is_far)
    def _():
        sequence(2, True)

    @pl.when(jnp.logical_not(on_plane))
    def _():
        sequence(9, False)

    for h in range(4):
        own_send(h, "wait")
        part_send(h, "wait")
    partner_piece.wait_send()
    partner_info.wait()
    for item in exchange:
        item.wait()


def update_kernel(
    place_ref, map_ref, info_ref, panel_ref, inv_ref, tiles_ref, rows_ref, cols_ref, recv_ref,
    factor_ref, out_ref, raw, left, right, in_sem, out_sem, fac_sem,
):
    held = out_ref.shape[0]
    load_left = pltpu.make_async_copy(rows_ref, left, fac_sem.at[0])
    load_right = pltpu.make_async_copy(cols_ref, right, fac_sem.at[1])
    load_left.start()
    load_right.start()

    def fetch(j):
        s = place_ref[j]

        @pl.when((s >= 0) & (s < 40))
        def _():
            pltpu.make_async_copy(
                tiles_ref.at[jnp.clip(s, 0, 39)], raw.at[j], in_sem.at[j]
            ).start()

        @pl.when(s >= 40)
        def _():
            pltpu.make_async_copy(
                recv_ref.at[jnp.clip(s - 40, 0, 5)], raw.at[j], in_sem.at[j]
            ).start()

    pl.loop(0, held)(fetch)
    factor_ref[...] = solve(panel_ref[...], inv_ref[...])
    load_left.wait()
    load_right.wait()

    def renew(j):
        s = place_ref[j]
        far = s >= 40
        near_slot = jnp.clip(s, 0, 39)
        far_slot = jnp.clip(s - 40, 0, 5)
        a = jnp.where(far, info_ref[far_slot, 0], map_ref[near_slot, 0])
        b = jnp.where(far, info_ref[far_slot, 1], map_ref[near_slot, 1])
        a = jnp.clip(a, 0, 3)
        b = jnp.clip(b, 0, 15)

        @pl.when(s >= 0)
        def _():
            pltpu.make_async_copy(tiles_ref.at[0], raw.at[j], in_sem.at[j]).wait()
            product = lax.dot_general(
                left[jnp.where(far, 4, 0) + a],
                right[(b % 4) * 4 + b // 4],
                (((1,), (1,)), ((), ())),
                preferred_element_type=jnp.float32,
            )
            raw[j] = (raw[j].astype(jnp.float32) - product).astype(jnp.bfloat16)

        @pl.when(s < 0)
        def _():
            raw[j] = jnp.zeros((256, 256), jnp.bfloat16)

        pltpu.make_async_copy(raw.at[j], out_ref.at[j], out_sem.at[j]).start()

    pl.loop(0, held)(renew)

    def finish(j):
        pltpu.make_async_copy(raw.at[j], out_ref.at[j], out_sem.at[j]).wait()

    pl.loop(0, held)(finish)


def shards(panel, diag_inverse, tiles, tile_map, send_list, place_list):
    vmem = pl.BlockSpec(memory_space=pltpu.VMEM)
    smem = pl.BlockSpec(memory_space=pltpu.SMEM)
    anyw = pl.BlockSpec(memory_space=pl.ANY)
    bf16 = jnp.bfloat16
    held = place_list.shape[0]
    rows, cols, recv, info = pl.pallas_call(
        gather_kernel,
        out_shape=(
            jax.ShapeDtypeStruct((16, 128, 256), bf16),
            jax.ShapeDtypeStruct((32, 128, 256), bf16),
            jax.ShapeDtypeStruct((6, 256, 256), bf16),
            jax.ShapeDtypeStruct((8, 128), jnp.int32),
        ),
        in_specs=[vmem, vmem, anyw, smem, smem],
        out_specs=(anyw, anyw, anyw, anyw),
        scratch_shapes=[
            pltpu.VMEM((40, 256, 256), bf16),
            pltpu.VMEM((6, 256, 256), bf16),
            pltpu.VMEM((128, 256), bf16),
            pltpu.VMEM((8, 128), jnp.int32),
            pltpu.SemaphoreType.DMA((SEND.count,)),
            pltpu.SemaphoreType.DMA((RECV.count,)),
            pltpu.SemaphoreType.DMA((3,)),
        ],
        compiler_params=pltpu.CompilerParams(
            collective_id=0, has_side_effects=True, vmem_limit_bytes=24 * 1024 * 1024
        ),
        name="gather_and_exchange",
    )(panel, diag_inverse, tiles, tile_map, send_list)
    left = rows.reshape(8, 256, 256)
    right = cols.reshape(16, 256, 256)
    return pl.pallas_call(
        update_kernel,
        out_shape=(
            jax.ShapeDtypeStruct((128, 256), jnp.float32),
            jax.ShapeDtypeStruct((held, 256, 256), bf16),
        ),
        in_specs=[smem, smem, smem, vmem, vmem, anyw, anyw, anyw, anyw],
        out_specs=(vmem, anyw),
        scratch_shapes=[
            pltpu.VMEM((held, 256, 256), bf16),
            pltpu.VMEM((8, 256, 256), bf16),
            pltpu.VMEM((16, 256, 256), bf16),
            pltpu.SemaphoreType.DMA((held,)),
            pltpu.SemaphoreType.DMA((held,)),
            pltpu.SemaphoreType.DMA((2,)),
        ],
        compiler_params=pltpu.CompilerParams(vmem_limit_bytes=24 * 1024 * 1024),
        name="update_and_place",
    )(place_list, tile_map, info, panel, diag_inverse, tiles, left, right, recv)


def solution(mesh):
    in_specs = (
        P(("row", "col"), None),
        P(),
        P(("row", "col"), None, None),
        P(("row", "col"), None),
        P(("row", "col")),
        P(("row", "col")),
    )
    out_specs = (P(("row", "col"), None), P(("row", "col"), None, None))
    return jax.shard_map(shards, mesh=mesh, in_specs=in_specs, out_specs=out_specs, check_vma=False)
```

time: 241 us -> 79.1 us (0.33)
  the two profiles are of different devices: /device:TPU:1 before, /device:TPU:2 now
where the time goes in v1:
time: 79.1 us; the launch traced here: 78.9 us
  Pallas kernels  72.5 us (92%)
  local copies, waits for them, and re-layouts  5.77 us (7%)
    pallas_call x1, Pallas kernels, shards(): pl.pallas_call(gather_kernel, out_shape=(jax.ShapeDtypeStruct((16, 128, 2...  54.1 us
    pallas_call x1, Pallas kernels, shards(): pl.pallas_call(update_kernel, out_shape=(jax.ShapeDtypeStruct((128, 256),...  18.4 us
    unnamed x11, local copies, waits for them, and re-layouts  5.77 us

profile of v1, /device:TPU:2, one launch (start us, length us, event | category | flops | bytes accessed | tf_op | source)
XLA Modules:
  0.0 78.9 jit_solution(724788898100024059)
XLA Ops:
  0.6 0.0 copy-start.4
  0.6 0.8 copy.9.map_ref
  1.4 0.0 copy-start
  1.4 2.5 %copy-done = bf16[40,256,256]{2,1,0:T(8,128)(2,1)S(1)} copy-done((bf16[40,256,256]{2,1,0:T(8,128)(2,1)S(1)}, bf16[40,256,256]{2,1,0:T(8,128)(2,1)}, u32[]{:S(2)}) %copy-start) | copy-done | bytes 5242904
  3.9 0.0 copy-start.1
  3.9 0.9 %copy-done.1 = f32[256,256]{1,0:T(8,128)S(1)} copy-done((f32[256,256]{1,0:T(8,128)S(1)}, f32[256,256]{1,0:T(8,128)}, u32[]{:S(2)}) %copy-start.1) | copy-done | bytes 262168
  4.8 0.0 copy-start.2
  4.8 0.9 %copy-done.2 = f32[128,256]{1,0:T(8,128)S(1)} copy-done((f32[128,256]{1,0:T(8,128)S(1)}, f32[128,256]{1,0:T(8,128)}, u32[]{:S(2)}) %copy-start.2) | copy-done | bytes 131096
  5.8 0.0 copy-start.3
  5.8 0.7 copy-done.3
  6.4 54.1 %gather_and_exchange.1 = (bf16[16,128,256]{2,1,0:T(8,128)(2,1)S(1)}, bf16[32,128,256]{2,1,0:T(8,128)(2,1)S(1)}, bf16[6,256,256]{2,1,0:T(8,128)(2,1)S(1)}, s32[8,128]{1,0:T(8,128)S(1)}) custom-call(f32[128,256]{1,0:T(8,128)S(1)} %copy-done.2, f32[256,256]{1,0:T(8,128)S(1)} %copy-done.1, bf16[40,256,256]{2,1,0:T(8,128)(2,1)S(1)} %copy-done, ...), custom_call_target="tpu_custom_call" | custom-call | tf_op jit(solution)/shard_map/gather_and_exchange/pallas_call | solution.py:369
  60.5 0.0 copy-done.4
  60.5 18.4 %update_and_place.1 = (f32[128,256]{1,0:T(8,128)}, bf16[34,256,256]{2,1,0:T(8,128)(2,1)}) custom-call(s32[34]{0:T(128)S(1)} %copy-done.4, s32[40,2]{1,0:T(8,128)S(1)} %copy.9.map_ref, s32[8,128]{1,0:T(8,128)S(1)} %get-tuple-element.6.info_ref, f32[128,256]{1,0:T(8,128)S(1)} %copy-done.2, f32[256,256]{1,0:T(8,128)S(1)} %copy-done.1, ...), custom_call_target="tpu_custom_call" | custom-call | tf_op jit(solution)/shard_map/update_and_place/pallas_call | solution.py:395
Async XLA Ops:
  0.6 59.9 %copy-start.4 = (s32[34]{0:T(128)S(1)}, s32[34]{0:T(128)}, u32[]{:S(2)}) copy-start(s32[34]{0:T(128)} %place_ref.1) | copy-start | bytes 412
  1.4 2.5 %copy-start = (bf16[40,256,256]{2,1,0:T(8,128)(2,1)S(1)}, bf16[40,256,256]{2,1,0:T(8,128)(2,1)}, u32[]{:S(2)}) copy-start(bf16[40,256,256]{2,1,0:T(8,128)(2,1)} %tiles_ref.3) | copy-start | bytes 15728644
  3.9 0.9 %copy-start.1 = (f32[256,256]{1,0:T(8,128)S(1)}, f32[256,256]{1,0:T(8,128)}, u32[]{:S(2)}) copy-start(f32[256,256]{1,0:T(8,128)} %inv_ref.3) | copy-start | bytes 786436
  4.8 0.9 %copy-start.2 = (f32[128,256]{1,0:T(8,128)S(1)}, f32[128,256]{1,0:T(8,128)}, u32[]{:S(2)}) copy-start(f32[128,256]{1,0:T(8,128)} %panel_ref.3) | copy-start | bytes 393220
  5.8 0.7 copy-start.3

commit v2 on v0

v2 whole, which is shorter than its diff:
```python
import functools

import jax
import jax.numpy as jnp
from jax import lax
from jax.experimental import pallas as pl
from jax.experimental.pallas import tpu as pltpu
from jax.sharding import PartitionSpec as P

MESH = pl.DeviceIdType.MESH
NX, NY, NZ = 4, 4, 8
PLACE = {0: 0, 1: 1, -1: 2, 2: 3, -2: 4, 3: 5, -3: 6, 4: 7, -4: 7}
HOPS = ((0, 1), (1, 2), (3, 2), (5, 2), (7, 1))
PARTS = ((0, 5, 2), (5, 3, 4))
PARTNER_TICK = 2
EXCHANGE_TICK = (0, 1, 2, 4, 6, 8)


class Ids:
    def __init__(self):
        self.count = 0

    def take(self, n):
        first = self.count
        self.count += n
        return first


SEND, RECV = Ids(), Ids()
S_ZP, S_ZM, S_QP, S_QM = (SEND.take(4) for _ in range(4))
S_PP, S_INFO = SEND.take(1), SEND.take(1)
S_EX = SEND.take(6)
S_YI, S_YC, S_YO, S_XC, S_XI, S_XF = (SEND.take(5) for _ in range(6))
S_DD = SEND.take(8)
R_ZP, R_ZM, R_QP, R_QM = (RECV.take(4) for _ in range(4))
R_PP, R_INFO = RECV.take(1), RECV.take(1)
R_EX = RECV.take(6)
R_AY, R_RC, R_RI, R_RF = (RECV.take(5) for _ in range(4))
R_DD = RECV.take(8)


def solve(panel, inverse):
    return lax.dot_general(
        panel,
        inverse,
        (((1,), (1,)), ((), ())),
        precision=lax.Precision.HIGHEST,
        preferred_element_type=jnp.float32,
    )


def product(left, right):
    return lax.dot_general(
        left, right, (((1,), (1,)), ((), ())), preferred_element_type=jnp.float32
    )


def panel_kernel(
    panel_hbm, inv_hbm, tiles_hbm, map_hbm, send_hbm,
    factor_ref, pool,
    panel_ref, inv_ref, map_ref, send_ref, rows_ref, cols_ref,
    send_buf, recv_buf, info_src, info_ref, info_at, send_sem, recv_sem, local_sem,
):
    r = lax.axis_index("row")
    z = lax.axis_index("col")
    x, y, k = r // 8, (r // 2) % 4, r % 2

    def dev(px, py, pk, pz):
        return (px * 8 + py * 2 + pk, pz)

    xi, xc = x + 1 - 2 * (x % 2), 3 - x
    yi, yc = y + 1 - 2 * (y % 2), 3 - y
    d_zp, d_zm = dev(x, y, k, (z + 1) % NZ), dev(x, y, k, (z + NZ - 1) % NZ)
    d_part = dev(3 - x, 3 - y, 1 - k, z)
    d_xi, d_xc = dev(xi, y, k, z), dev(xc, y, k, z)
    d_yi, d_yc = dev(x, yi, k, z), dev(x, yc, k, z)
    d_core = dev(x, y, 1 - k, z)
    sy, sk = z // 2, z % 2

    barrier = pltpu.get_barrier_semaphore()
    friends = (d_zp, d_zm, d_part, d_xi, d_xc, d_yi, d_yc, d_core)
    for friend in friends:
        pl.semaphore_signal(barrier, inc=1, device_id=friend, device_id_type=MESH)

    def local(src, dst, i):
        return pltpu.make_async_copy(src, dst, local_sem.at[i])

    load_panel = local(panel_hbm, panel_ref, 0)
    load_inv = local(inv_hbm, inv_ref, 1)
    load_map = local(map_hbm, map_ref, 2)
    load_send = local(send_hbm, send_ref, 3)
    load_tiles = local(tiles_hbm, pool.at[pl.ds(0, 40)], 4)
    for item in (load_panel, load_inv, load_map, load_send, load_tiles):
        item.start()
    load_panel.wait()
    load_inv.wait()
    factor = solve(panel_ref[...], inv_ref[...])
    factor_ref[...] = factor
    rows_ref[0] = factor.astype(jnp.bfloat16)

    def copy(src, dst, s, t, device):
        return pltpu.make_async_remote_copy(
            src_ref=src, dst_ref=dst, send_sem=send_sem.at[s], recv_sem=recv_sem.at[t],
            device_id=device, device_id_type=MESH,
        )

    def ring(base, h, up, s0, t0):
        sign = -1 if up else 1
        src, dst = base + PLACE[sign * h], base + PLACE[sign * (h + 1)]
        device = d_zp if up else d_zm
        if h < 3:
            return copy(rows_ref.at[src], rows_ref.at[dst], s0 + h, t0 + h, device)
        part = pl.ds(0, 64) if up else pl.ds(64, 64)
        return copy(rows_ref.at[src, part], rows_ref.at[dst, part], s0 + h, t0 + h, device)

    def ring_wait_recv(base, h, r_up, r_down):
        for sign, t, part in ((-1, r_up, pl.ds(0, 64)), (1, r_down, pl.ds(64, 64))):
            at = rows_ref.at[base + PLACE[sign * h]]
            if h == 4:
                at = rows_ref.at[base + PLACE[4], part]
            copy(at, at, 0, t + h - 1, d_zp).wait_recv()

    def own_hop(h):
        return (ring(0, h, True, S_ZP, R_ZP), ring(0, h, False, S_ZM, R_ZM))

    def part_hop(h):
        return (ring(8, h, True, S_QP, R_QP), ring(8, h, False, S_QM, R_QM))

    def start(copies):
        for item in copies:
            item.start()

    partner_piece = copy(rows_ref.at[0], rows_ref.at[8], S_PP, R_PP, d_part)
    partner_info = copy(info_src, info_ref, S_INFO, R_INFO, d_part)
    exchange = [
        copy(send_buf.at[j], recv_buf.at[j], S_EX + j, R_EX + j, d_part) for j in range(6)
    ]

    def cols_at(block, g):
        return cols_ref.at[pl.ds(block * 8 + HOPS[g][0], HOPS[g][1])]

    def mine(g, source):
        return rows_ref.at[pl.ds(*HOPS[g])] if source else cols_at(x, g)

    def y_in(g, source):
        return copy(mine(g, source), cols_at(x, g), S_YI + g, R_AY + g, d_yi)

    def y_cross(g, source):
        return copy(mine(g, source), cols_at(x, g), S_YC + g, R_AY + g, d_yc)

    def y_over(g):
        return copy(cols_at(x, g), cols_at(x, g), S_YO + g, R_AY + g, d_yi)

    def x_cross(g, source):
        return copy(mine(g, source), cols_at(x, g), S_XC + g, R_RC + g, d_xc)

    def x_in(g, source):
        return copy(mine(g, source), cols_at(x, g), S_XI + g, R_RI + g, d_xi)

    def x_forward(g):
        return copy(cols_at(xc, g), cols_at(xc, g), S_XF + g, R_RF + g, d_xi)

    def to_core(which, p, source):
        block = (x, xc, xi, 3 - xi)[which]
        first, count, _ = PARTS[p]
        dst = cols_ref.at[pl.ds(block * 8 + first, count)]
        src = rows_ref.at[pl.ds(first, count)] if source and which == 0 else dst
        return copy(src, dst, S_DD + which * 2 + p, R_DD + which * 2 + p, d_core)

    def pass_on(which, g, source):
        for p in range(2):
            if PARTS[p][2] == g:
                to_core(which, p, source).start()

    def arrived(ref, t):
        copy(ref, ref, 0, t, d_core).wait_recv()

    pl.semaphore_wait(barrier, len(friends))
    start(own_hop(0))
    partner_piece.start()
    load_map.wait()
    load_send.wait()
    load_tiles.wait()
    lane = lax.broadcasted_iota(jnp.int32, (8, 128), 1)
    sub = lax.broadcasted_iota(jnp.int32, (8, 128), 0)
    info = jnp.zeros((8, 128), jnp.int32)
    for j in range(6):
        slot = jnp.clip(send_ref[j], 0, 39)
        send_buf[j] = pool[slot]
        info = jnp.where((sub == j) & (lane == 0), map_ref[0, slot], info)
        info = jnp.where((sub == j) & (lane == 1), map_ref[1, slot], info)
    info_src[...] = info
    partner_info.start()


    def sequence(depth, plane):
        source = depth == 0
        for t in range(0, 9):
            for j in range(6):
                if EXCHANGE_TICK[j] == t:
                    exchange[j].start()
            if 1 <= t <= 4:
                ring_wait_recv(0, t, R_ZP, R_ZM)
                if t <= 3:
                    start(own_hop(t))
            p = t - PARTNER_TICK
            if p == 0:
                partner_piece.wait_recv()
                start(part_hop(0))
            elif 1 <= p <= 4:
                ring_wait_recv(8, p, R_QP, R_QM)
                if p <= 3:
                    start(part_hop(p))
            if not plane:
                continue
            g = t - depth
            if 0 <= g <= 4:
                if source:
                    y_cross(g, source).start()
                    y_in(g, source).start()
                else:
                    arrived(cols_at(x, g), R_AY + g)
                if depth == 1:
                    @pl.when(y == 3 - sy)
                    def _():
                        y_over(g).start()
                x_cross(g, source).start()
                x_in(g, source).start()
                pass_on(0, g, source)
            g = t - depth - 1
            if 0 <= g <= 4:
                arrived(cols_at(xc, g), R_RC + g)
                x_forward(g).start()
                pass_on(1, g, source)
                arrived(cols_at(xi, g), R_RI + g)
                pass_on(2, g, source)
            g = t - depth - 2
            if 0 <= g <= 4:
                arrived(cols_at(3 - xi, g), R_RF + g)
                pass_on(3, g, source)
        if source:
            for i in range(8):
                cols_ref[x * 8 + i] = rows_ref[i]
        if plane:
            for g in range(5):
                if source:
                    y_in(g, source).wait_send()
                    y_cross(g, source).wait_send()
                if depth == 1:
                    @pl.when(y == 3 - sy)
                    def _():
                        y_over(g).wait_send()
                x_cross(g, source).wait_send()
                x_in(g, source).wait_send()
                x_forward(g).wait_send()
            for which in range(4):
                for p in range(2):
                    to_core(which, p, source).wait_send()
        else:
            for which in range(4):
                for p in range(2):
                    to_core(which, p, False).wait_recv()

    on_plane = k == sk
    is_source = y == sy
    is_far = y == (3 - sy) + 1 - 2 * ((3 - sy) % 2)

    @pl.when(on_plane & is_source)
    def _():
        sequence(0, True)

    @pl.when(on_plane & jnp.logical_not(is_source) & jnp.logical_not(is_far))
    def _():
        sequence(1, True)

    @pl.when(on_plane & is_far)
    def _():
        sequence(2, True)

    @pl.when(jnp.logical_not(on_plane))
    def _():
        sequence(9, False)


    def both_halves(ref, base, tile):
        def half(at):
            off = lax.rem(at - z + NZ, NZ)
            return ref[base + jnp.where(off <= 4, jnp.maximum(2 * off - 1, 0), 2 * (NZ - off))]

        return jnp.concatenate([half(2 * tile), half(2 * tile + 1)], 0)

    def factors(a, b, far):
        a = jnp.clip(a, 0, 3)
        b = jnp.clip(b, 0, 15)
        return product(both_halves(rows_ref, 8 * far, a), both_halves(cols_ref, (b % 4) * 8, b // 4))

    def renew(raw, first, count, parts):
        for u in range(count):
            value = raw(u).astype(jnp.float32) - parts[u]
            pool[first + u] = value.astype(jnp.bfloat16)

    @pl.loop(0, 5)
    def _(q):
        parts = [factors(map_ref[0, q * 8 + u], map_ref[1, q * 8 + u], 0) for u in range(8)]
        renew(lambda u: pool[q * 8 + u], q * 8, 8, parts)

    partner_info.wait()
    place_info = local(info_ref, info_at, 2)
    place_info.start()
    place_info.wait()
    for item in exchange:
        item.wait()
    parts = [factors(info_at[u, 0], info_at[u, 1], 1) for u in range(6)]
    renew(lambda u: recv_buf[u], 40, 6, parts)
    for h in range(4):
        for item in own_hop(h) + part_hop(h):
            item.wait_send()
    partner_piece.wait_send()


def place_kernel(place_ref, pool_ref, factor_in, factor_out, out_ref, zeros, sem, factor_sem):
    held = out_ref.shape[0]
    factor_copy = pltpu.make_async_copy(factor_in, factor_out, factor_sem)
    factor_copy.start()
    zeros[...] = jnp.zeros_like(zeros)

    @pl.loop(0, held)
    def _(j):
        s = place_ref[j]

        @pl.when(s >= 0)
        def _():
            pltpu.make_async_copy(pool_ref.at[jnp.clip(s, 0, 45)], out_ref.at[j], sem.at[j]).start()

        @pl.when(s < 0)
        def _():
            pltpu.make_async_copy(zeros, out_ref.at[j], sem.at[j]).start()

    @pl.loop(0, held)
    def _(j):
        pltpu.make_async_copy(zeros, out_ref.at[j], sem.at[j]).wait()

    factor_copy.wait()


def shards(panel, diag_inverse, tiles, tile_map, send_list, place_list):
    vmem = pl.BlockSpec(memory_space=pltpu.VMEM)
    smem = pl.BlockSpec(memory_space=pltpu.SMEM)
    hbm = pl.BlockSpec(memory_space=pltpu.HBM)
    bf16 = jnp.bfloat16
    held = place_list.shape[0]
    factor, pool = pl.pallas_call(
        panel_kernel,
        out_shape=(
            pltpu.VMEM((128, 256), jnp.float32),
            pltpu.VMEM((46, 256, 256), bf16),
        ),
        in_specs=[hbm] * 5,
        out_specs=(vmem, vmem),
        scratch_shapes=[
            pltpu.VMEM((128, 256), jnp.float32),
            pltpu.VMEM((256, 256), jnp.float32),
            pltpu.SMEM((2, 40), jnp.int32),
            pltpu.SMEM((6,), jnp.int32),
            pltpu.VMEM((16, 128, 256), bf16),
            pltpu.VMEM((32, 128, 256), bf16),
            pltpu.VMEM((6, 256, 256), bf16),
            pltpu.VMEM((6, 256, 256), bf16),
            pltpu.VMEM((8, 128), jnp.int32),
            pltpu.VMEM((8, 128), jnp.int32),
            pltpu.SMEM((8, 128), jnp.int32),
            pltpu.SemaphoreType.DMA((SEND.count,)),
            pltpu.SemaphoreType.DMA((RECV.count,)),
            pltpu.SemaphoreType.DMA((5,)),
        ],
        compiler_params=pltpu.CompilerParams(
            collective_id=0, has_side_effects=True, vmem_limit_bytes=54 * 1024 * 1024
        ),
        name="gather_exchange_renew",
    )(panel, diag_inverse, tiles, tile_map.T, send_list)
    return pl.pallas_call(
        place_kernel,
        out_shape=(
            jax.ShapeDtypeStruct((128, 256), jnp.float32),
            jax.ShapeDtypeStruct((held, 256, 256), bf16),
        ),
        in_specs=[smem, pl.BlockSpec(memory_space=pl.ANY), pl.BlockSpec(memory_space=pl.ANY)],
        out_specs=(hbm, hbm),
        scratch_shapes=[
            pltpu.VMEM((256, 256), bf16),
            pltpu.SemaphoreType.DMA((held,)),
            pltpu.SemaphoreType.DMA,
        ],
        compiler_params=pltpu.CompilerParams(vmem_limit_bytes=4 * 1024 * 1024),
        name="place",
    )(place_list, pool, factor)


def solution(mesh):
    in_specs = (
        P(("row", "col"), None),
        P(),
        P(("row", "col"), None, None),
        P(("row", "col"), None),
        P(("row", "col")),
        P(("row", "col")),
    )
    out_specs = (P(("row", "col"), None), P(("row", "col"), None, None))
    return jax.shard_map(shards, mesh=mesh, in_specs=in_specs, out_specs=out_specs, check_vma=False)
```

time: 241 us -> 50.3 us (0.21)
  the two profiles are of different devices: /device:TPU:1 before, /device:TPU:19 now
where the time goes in v2:
time: 50.3 us; the launch traced here: 50.2 us
  Pallas kernels  49.6 us (99%)
  between operations  0.66 us (1%)
    pallas_call x1, Pallas kernels, shards(): pl.pallas_call(panel_kernel, out_shape=(pltpu.VMEM((128, 256), jnp.float3...  46.6 us
    pallas_call x1, Pallas kernels, shards(): pl.pallas_call(place_kernel, out_shape=(jax.ShapeDtypeStruct((128, 256),...  2.95 us

profile of v2, /device:TPU:19, one launch (start us, length us, event | category | flops | bytes accessed | tf_op | source)
XLA Modules:
  0.0 50.2 jit_solution(15828839398376336880)
XLA Ops:
  0.6 0.0 copy-start
  0.6 46.6 %gather_exchange_renew.1 = (f32[128,256]{1,0:T(8,128)S(1)}, bf16[46,256,256]{2,1,0:T(8,128)(2,1)S(1)}) custom-call(f32[128,256]{1,0:T(8,128)} %panel_hbm.1, f32[256,256]{1,0:T(8,128)} %inv_hbm.1, bf16[40,256,256]{2,1,0:T(8,128)(2,1)} %tiles_hbm.1, s32[2,40]{1,0:T(2,128)} %bitcast.1, s32[6]{0:T(128)} %send_hbm.1), custom_call_target="tpu_custom_call" | custom-call | tf_op jit(solution)/shard_map/gather_exchange_renew/pallas_call | solution.py:352
  47.2 0.0 copy-done
  47.3 3.0 %place.1 = (f32[128,256]{1,0:T(8,128)}, bf16[34,256,256]{2,1,0:T(8,128)(2,1)}) custom-call(s32[34]{0:T(128)S(1)} %copy-done, bf16[46,256,256]{2,1,0:T(8,128)(2,1)S(1)} %get-tuple-element.4.pool_ref, f32[128,256]{1,0:T(8,128)S(1)} %get-tuple-element.5.factor_in), custom_call_target="tpu_custom_call" | custom-call | tf_op jit(solution)/shard_map/place/pallas_call | solution.py:381
Async XLA Ops:
  0.6 46.6 %copy-start = (s32[34]{0:T(128)S(1)}, s32[34]{0:T(128)}, u32[]{:S(2)}) copy-start(s32[34]{0:T(128)} %place_ref.1) | copy-start | bytes 412

commit v3 on v2

--- a/solution.py
+++ b/solution.py
@@ -75,10 +75,11 @@
     d_xi, d_xc = dev(xi, y, k, z), dev(xc, y, k, z)
     d_yi, d_yc = dev(x, yi, k, z), dev(x, yc, k, z)
     d_core = dev(x, y, 1 - k, z)
+    d_far = dev(x, 3 - yi, k, z)
     sy, sk = z // 2, z % 2
 
     barrier = pltpu.get_barrier_semaphore()
-    friends = (d_zp, d_zm, d_part, d_xi, d_xc, d_yi, d_yc, d_core)
+    friends = (d_zp, d_zm, d_part, d_xi, d_xc, d_yi, d_yc, d_far, d_core)
     for friend in friends:
         pl.semaphore_signal(barrier, inc=1, device_id=friend, device_id_type=MESH)
 
@@ -149,7 +150,7 @@
         return copy(mine(g, source), cols_at(x, g), S_YC + g, R_AY + g, d_yc)
 
     def y_over(g):
-        return copy(cols_at(x, g), cols_at(x, g), S_YO + g, R_AY + g, d_yi)
+        return copy(mine(g, True), cols_at(x, g), S_YO + g, R_AY + g, d_far)
 
     def x_cross(g, source):
         return copy(mine(g, source), cols_at(x, g), S_XC + g, R_RC + g, d_xc)
@@ -217,13 +218,10 @@
             if 0 <= g <= 4:
                 if source:
                     y_cross(g, source).start()
+                    y_over(g).start()
                     y_in(g, source).start()
                 else:
                     arrived(cols_at(x, g), R_AY + g)
-                if depth == 1:
-                    @pl.when(y == 3 - sy)
-                    def _():
-                        y_over(g).start()
                 x_cross(g, source).start()
                 x_in(g, source).start()
                 pass_on(0, g, source)
@@ -245,11 +243,8 @@
             for g in range(5):
                 if source:
                     y_in(g, source).wait_send()
+                    y_over(g).wait_send()
                     y_cross(g, source).wait_send()
-                if depth == 1:
-                    @pl.when(y == 3 - sy)
-                    def _():
-                        y_over(g).wait_send()
                 x_cross(g, source).wait_send()
                 x_in(g, source).wait_send()
                 x_forward(g).wait_send()
@@ -275,7 +270,7 @@
 
     @pl.when(on_plane & is_far)
     def _():
-        sequence(2, True)
+        sequence(1, True)
 
     @pl.when(jnp.logical_not(on_plane))
     def _():

time: 50.3 us -> 48 us (0.954)
  the two profiles are of different devices: /device:TPU:19 before, /device:TPU:1 now
where the time goes in v3:
time: 48 us; the launch traced here: 47.9 us
  Pallas kernels  47.3 us (99%)
  between operations  0.66 us (1%)
    pallas_call x1, Pallas kernels, shards(): pl.pallas_call(panel_kernel, out_shape=(pltpu.VMEM((128, 256), jnp.float3...  44.3 us
    pallas_call x1, Pallas kernels, shards(): pl.pallas_call(place_kernel, out_shape=(jax.ShapeDtypeStruct((128, 256),...  2.95 us

profile of v3, /device:TPU:1, one launch (start us, length us, event | category | flops | bytes accessed | tf_op | source)
XLA Modules:
  0.0 47.9 jit_solution(3941764979966811493)
XLA Ops:
  0.6 0.0 copy-start
  0.6 44.3 %gather_exchange_renew.1 = (f32[128,256]{1,0:T(8,128)S(1)}, bf16[46,256,256]{2,1,0:T(8,128)(2,1)S(1)}) custom-call(f32[128,256]{1,0:T(8,128)} %panel_hbm.1, f32[256,256]{1,0:T(8,128)} %inv_hbm.1, bf16[40,256,256]{2,1,0:T(8,128)(2,1)} %tiles_hbm.1, s32[2,40]{1,0:T(2,128)} %bitcast.1, s32[6]{0:T(128)} %send_hbm.1), custom_call_target="tpu_custom_call" | custom-call | tf_op jit(solution)/shard_map/gather_exchange_renew/pallas_call | solution.py:347
  45.0 0.0 copy-done
  45.0 3.0 %place.1 = (f32[128,256]{1,0:T(8,128)}, bf16[34,256,256]{2,1,0:T(8,128)(2,1)}) custom-call(s32[34]{0:T(128)S(1)} %copy-done, bf16[46,256,256]{2,1,0:T(8,128)(2,1)S(1)} %get-tuple-element.4.pool_ref, f32[128,256]{1,0:T(8,128)S(1)} %get-tuple-element.5.factor_in), custom_call_target="tpu_custom_call" | custom-call | tf_op jit(solution)/shard_map/place/pallas_call | solution.py:376
Async XLA Ops:
  0.6 44.4 %copy-start = (s32[34]{0:T(128)S(1)}, s32[34]{0:T(128)}, u32[]{:S(2)}) copy-start(s32[34]{0:T(128)} %place_ref.1) | copy-start | bytes 412

commit v4 on v3

--- a/solution.py
+++ b/solution.py
@@ -11,7 +11,6 @@
 NX, NY, NZ = 4, 4, 8
 PLACE = {0: 0, 1: 1, -1: 2, 2: 3, -2: 4, 3: 5, -3: 6, 4: 7, -4: 7}
 HOPS = ((0, 1), (1, 2), (3, 2), (5, 2), (7, 1))
-PARTS = ((0, 5, 2), (5, 3, 4))
 PARTNER_TICK = 2
 EXCHANGE_TICK = (0, 1, 2, 4, 6, 8)
 
@@ -31,12 +30,12 @@
 S_PP, S_INFO = SEND.take(1), SEND.take(1)
 S_EX = SEND.take(6)
 S_YI, S_YC, S_YO, S_XC, S_XI, S_XF = (SEND.take(5) for _ in range(6))
-S_DD = SEND.take(8)
+S_DD = SEND.take(20)
 R_ZP, R_ZM, R_QP, R_QM = (RECV.take(4) for _ in range(4))
 R_PP, R_INFO = RECV.take(1), RECV.take(1)
 R_EX = RECV.take(6)
 R_AY, R_RC, R_RI, R_RF = (RECV.take(5) for _ in range(4))
-R_DD = RECV.take(8)
+R_DD = RECV.take(20)
 
 
 def solve(panel, inverse):
@@ -75,11 +74,15 @@
     d_xi, d_xc = dev(xi, y, k, z), dev(xc, y, k, z)
     d_yi, d_yc = dev(x, yi, k, z), dev(x, yc, k, z)
     d_core = dev(x, y, 1 - k, z)
+    full = (r >= 24) & (r - 24 >= z)
+    far_r = 31 - r
+    partner_full = (far_r >= 24) & (far_r - 24 >= z)
+    d_xo = dev(3 - xi, y, k, z)
     d_far = dev(x, 3 - yi, k, z)
     sy, sk = z // 2, z % 2
 
     barrier = pltpu.get_barrier_semaphore()
-    friends = (d_zp, d_zm, d_part, d_xi, d_xc, d_yi, d_yc, d_far, d_core)
+    friends = (d_zp, d_zm, d_part, d_xi, d_xc, d_yi, d_yc, d_far, d_xo, d_core)
     for friend in friends:
         pl.semaphore_signal(barrier, inc=1, device_id=friend, device_id_type=MESH)
 
@@ -158,20 +161,13 @@
     def x_in(g, source):
         return copy(mine(g, source), cols_at(x, g), S_XI + g, R_RI + g, d_xi)
 
-    def x_forward(g):
-        return copy(cols_at(xc, g), cols_at(xc, g), S_XF + g, R_RF + g, d_xi)
-
-    def to_core(which, p, source):
+    def x_over(g, source):
+        return copy(mine(g, source), cols_at(x, g), S_XF + g, R_RF + g, d_xo)
+
+    def to_core(which, g, source):
         block = (x, xc, xi, 3 - xi)[which]
-        first, count, _ = PARTS[p]
-        dst = cols_ref.at[pl.ds(block * 8 + first, count)]
-        src = rows_ref.at[pl.ds(first, count)] if source and which == 0 else dst
-        return copy(src, dst, S_DD + which * 2 + p, R_DD + which * 2 + p, d_core)
-
-    def pass_on(which, g, source):
-        for p in range(2):
-            if PARTS[p][2] == g:
-                to_core(which, p, source).start()
+        src = mine(g, source) if which == 0 else cols_at(block, g)
+        return copy(src, cols_at(block, g), S_DD + which * 5 + g, R_DD + which * 5 + g, d_core)
 
     def arrived(ref, t):
         copy(ref, ref, 0, t, d_core).wait_recv()
@@ -196,10 +192,10 @@
 
     def sequence(depth, plane):
         source = depth == 0
-        for t in range(0, 9):
+        for t in range(0, 10):
             for j in range(6):
                 if EXCHANGE_TICK[j] == t:
-                    exchange[j].start()
+                    pl.when(jnp.logical_not(partner_full))(exchange[j].start)
             if 1 <= t <= 4:
                 ring_wait_recv(0, t, R_ZP, R_ZM)
                 if t <= 3:
@@ -223,19 +219,19 @@
                 else:
                     arrived(cols_at(x, g), R_AY + g)
                 x_cross(g, source).start()
+                x_over(g, source).start()
                 x_in(g, source).start()
-                pass_on(0, g, source)
-            g = t - depth - 1
+                to_core(0, g, source).start()
+            g = t - depth - 2
             if 0 <= g <= 4:
                 arrived(cols_at(xc, g), R_RC + g)
-                x_forward(g).start()
-                pass_on(1, g, source)
+                to_core(1, g, source).start()
                 arrived(cols_at(xi, g), R_RI + g)
-                pass_on(2, g, source)
+                to_core(2, g, source).start()
             g = t - depth - 2
             if 0 <= g <= 4:
                 arrived(cols_at(3 - xi, g), R_RF + g)
-                pass_on(3, g, source)
+                to_core(3, g, source).start()
         if source:
             for i in range(8):
                 cols_ref[x * 8 + i] = rows_ref[i]
@@ -247,14 +243,14 @@
                     y_cross(g, source).wait_send()
                 x_cross(g, source).wait_send()
                 x_in(g, source).wait_send()
-                x_forward(g).wait_send()
+                x_over(g, source).wait_send()
             for which in range(4):
-                for p in range(2):
-                    to_core(which, p, source).wait_send()
+                for g in range(5):
+                    to_core(which, g, source).wait_send()
         else:
             for which in range(4):
-                for p in range(2):
-                    to_core(which, p, False).wait_recv()
+                for g in range(5):
+                    to_core(which, g, False).wait_recv()
 
     on_plane = k == sk
     is_source = y == sy
@@ -303,10 +299,18 @@
     place_info = local(info_ref, info_at, 2)
     place_info.start()
     place_info.wait()
-    for item in exchange:
-        item.wait()
-    parts = [factors(info_at[u, 0], info_at[u, 1], 1) for u in range(6)]
-    renew(lambda u: recv_buf[u], 40, 6, parts)
+    @pl.when(jnp.logical_not(full))
+    def _():
+        for item in exchange:
+            item.wait_recv()
+        parts = [factors(info_at[u, 0], info_at[u, 1], 1) for u in range(6)]
+        renew(lambda u: recv_buf[u], 40, 6, parts)
+
+    @pl.when(jnp.logical_not(partner_full))
+    def _():
+        for item in exchange:
+            item.wait_send()
+
     for h in range(4):
         for item in own_hop(h) + part_hop(h):
             item.wait_send()

time: 48 us -> 47.5 us (0.990)
  Pallas kernels: 47.3 us -> 46.7 us
    pallas_call x1, Pallas kernels: 44.3 us -> 43.8 us  [shards(): pl.pallas_call(panel_kernel, out_shape=(pltpu.VMEM((128, 256), jnp.float3...]
where the time goes in v4:
time: 47.5 us; the launch traced here: 47.4 us
  Pallas kernels  46.7 us (98%)
  between operations  0.66 us (1%)
    pallas_call x1, Pallas kernels, shards(): pl.pallas_call(panel_kernel, out_shape=(pltpu.VMEM((128, 256), jnp.float3...  43.8 us
    pallas_call x1, Pallas kernels, shards(): pl.pallas_call(place_kernel, out_shape=(jax.ShapeDtypeStruct((128, 256),...  2.95 us

profile of v4, /device:TPU:1, one launch (start us, length us, event | category | flops | bytes accessed | tf_op | source)
XLA Modules:
  0.0 47.4 jit_solution(15459524676105220909)
XLA Ops:
  0.6 0.0 copy-start
  0.6 43.8 %gather_exchange_renew.1 = (f32[128,256]{1,0:T(8,128)S(1)}, bf16[46,256,256]{2,1,0:T(8,128)(2,1)S(1)}) custom-call(f32[128,256]{1,0:T(8,128)} %panel_hbm.1, f32[256,256]{1,0:T(8,128)} %inv_hbm.1, bf16[40,256,256]{2,1,0:T(8,128)(2,1)} %tiles_hbm.1, s32[2,40]{1,0:T(2,128)} %bitcast.1, s32[6]{0:T(128)} %send_hbm.1), custom_call_target="tpu_custom_call" | custom-call | tf_op jit(solution)/shard_map/gather_exchange_renew/pallas_call | solution.py:351
  44.4 0.0 copy-done
  44.4 3.0 %place.1 = (f32[128,256]{1,0:T(8,128)}, bf16[34,256,256]{2,1,0:T(8,128)(2,1)}) custom-call(s32[34]{0:T(128)S(1)} %copy-done, bf16[46,256,256]{2,1,0:T(8,128)(2,1)S(1)} %get-tuple-element.4.pool_ref, f32[128,256]{1,0:T(8,128)S(1)} %get-tuple-element.5.factor_in), custom_call_target="tpu_custom_call" | custom-call | tf_op jit(solution)/shard_map/place/pallas_call | solution.py:380
Async XLA Ops:
  0.6 43.8 %copy-start = (s32[34]{0:T(128)S(1)}, s32[34]{0:T(128)}, u32[]{:S(2)}) copy-start(s32[34]{0:T(128)} %place_ref.1) | copy-start | bytes 412

commit v5 on v4

--- a/solution.py
+++ b/solution.py
@@ -12,7 +12,7 @@
 PLACE = {0: 0, 1: 1, -1: 2, 2: 3, -2: 4, 3: 5, -3: 6, 4: 7, -4: 7}
 HOPS = ((0, 1), (1, 2), (3, 2), (5, 2), (7, 1))
 PARTNER_TICK = 2
-EXCHANGE_TICK = (0, 1, 2, 4, 6, 8)
+EXCHANGE_TICK = (0, 1, 2, 4, 5, 7)
 
 
 class Ids:

time: 47.5 us -> 47.7 us (level)
  no operation moved by 1% of the time
where the time goes in v5:
time: 47.7 us; the launch traced here: 47.6 us
  Pallas kernels  46.9 us (98%)
  between operations  0.66 us (1%)
    pallas_call x1, Pallas kernels, shards(): pl.pallas_call(panel_kernel, out_shape=(pltpu.VMEM((128, 256), jnp.float3...  44 us
    pallas_call x1, Pallas kernels, shards(): pl.pallas_call(place_kernel, out_shape=(jax.ShapeDtypeStruct((128, 256),...  2.95 us

profile of v5, /device:TPU:1, one launch (start us, length us, event | category | flops | bytes accessed | tf_op | source)
XLA Modules:
  0.0 47.6 jit_solution(1643776147690919520)
XLA Ops:
  0.6 0.0 copy-start
  0.6 44.0 %gather_exchange_renew.1 = (f32[128,256]{1,0:T(8,128)S(1)}, bf16[46,256,256]{2,1,0:T(8,128)(2,1)S(1)}) custom-call(f32[128,256]{1,0:T(8,128)} %panel_hbm.1, f32[256,256]{1,0:T(8,128)} %inv_hbm.1, bf16[40,256,256]{2,1,0:T(8,128)(2,1)} %tiles_hbm.1, s32[2,40]{1,0:T(2,128)} %bitcast.1, s32[6]{0:T(128)} %send_hbm.1), custom_call_target="tpu_custom_call" | custom-call | tf_op jit(solution)/shard_map/gather_exchange_renew/pallas_call | solution.py:351
  44.6 0.0 copy-done
  44.6 3.0 %place.1 = (f32[128,256]{1,0:T(8,128)}, bf16[34,256,256]{2,1,0:T(8,128)(2,1)}) custom-call(s32[34]{0:T(128)S(1)} %copy-done, bf16[46,256,256]{2,1,0:T(8,128)(2,1)S(1)} %get-tuple-element.4.pool_ref, f32[128,256]{1,0:T(8,128)S(1)} %get-tuple-element.5.factor_in), custom_call_target="tpu_custom_call" | custom-call | tf_op jit(solution)/shard_map/place/pallas_call | solution.py:380
Async XLA Ops:
  0.6 44.0 %copy-start = (s32[34]{0:T(128)S(1)}, s32[34]{0:T(128)}, u32[]{:S(2)}) copy-start(s32[34]{0:T(128)} %place_ref.1) | copy-start | bytes 412
